TPU v7x, 32 devices: a whole 2x2x4 slice. The times are simulated.
32 devices in a mesh: req: 8 (over z, x), tp: 4 (over y, core).
Axes of the slice: x: 2, y: 2, z: 4, core: 2. Of those that a mesh axis runs over, the one named last changes fastest.
Arguments:
- layer_in: bfloat16 [4, 64, 2880], P(None, 'req'), may hold values from -3 to 3
- query_in: bfloat16 [4, 64, 2048], P(None, 'req', 'tp'), may hold values from -6 to 6
- unrotated_key: bfloat16 [4, 64, 512], P(None, 'req', 'tp'), may hold values from -6 to 6
- incoming_value: bfloat16 [4, 64, 512], P(None, 'req', 'tp'), may hold values from -12 to 12
- rotated_prompt_keys: bfloat16 [64, 256, 512], P('req', None, 'tp'), may hold values from -270 to 270
- prompt_value_rows: bfloat16 [64, 256, 512], P('req', None, 'tp'), may hold values from -6 to 6
- generated_key_rows: bfloat16 [64, 64, 512], P('req', None, 'tp'), may hold values from -9 to 9
- generated_value_rows: bfloat16 [64, 64, 512], P('req', None, 'tp'), may hold values from -12 to 12
- lengths: int32 [8], replicated, may hold values from 128 to 2048, as said below
- parents: int32 [4, 8, 8], replicated, may hold values from 0 to 7
- routes: int32 [4, 64, 4], P(None, 'req'), may hold values from 0 to 15, all different within a row; in each aligned block of 8 rows (0 to 7, 8 to 15, ..., all dimensions but the last counted through in order) at most 4 rows name the same one
- head_sink_logits: float32 [32], P('tp'), may hold values from 1 to 6
- out_weight: bfloat16 [2048, 2880], P('tp'), may hold values from -0.5 to 0.5
- mlp_gain: float32 [2880], replicated, may hold values from 0.5 to 1.5
- router_weight: bfloat16 [2880, 16], replicated, may hold values from -0.21875 to 0.21875
- expert_gate: bfloat16 [16, 2880, 2880], P('req', None, 'tp'), may hold values from -0.4375 to 0.4375
- expert_up: bfloat16 [16, 2880, 2880], P('req', None, 'tp'), may hold values from -0.4375 to 0.4375
- expert_down: bfloat16 [16, 2880, 2880], P('req', 'tp'), may hold values from -0.109375 to 0.109375
- next_gain: float32 [2880], replicated, may hold values from 0.5 to 1.5
- next_q_weight: bfloat16 [2880, 2048], P(None, 'tp'), may hold values from -0.109375 to 0.109375
- following_key_value_weight: bfloat16 [2880, 2, 512], P(None, None, 'tp'), may hold values from -0.109375 to 0.109375
Outputs:
- layer_out: bfloat16 [4, 64, 2880], P(None, 'req')
- next_query: bfloat16 [4, 64, 2048], P(None, 'req', 'tp')
- next_keyval: bfloat16 [4, 64, 2, 512], P(None, 'req', None, 'tp')
Inputs may be any that keep to these rules, and one draw needn't show every extreme that they name: `lengths`: some group's prompt holds exactly 2048 positions. `routes`: a row names 4 different experts; in the rows of one device at one step no expert is named more than 4 times, a bound that some block reaches.
All inputs are finite; a program needn't handle non-finite values.
Results may differ from a plain program's by a relative error of at most 0.029.
Values may be sent and summed in bfloat16 or wider, within the bound.
A program may use at most 128 MiB of HBM per device.

v0:
```python
import jax
import jax.numpy as jnp
from jax import lax
from jax.sharding import PartitionSpec as P

HEAD = 64
EXPERTS = 16
THETA = 150000.0
EPS = 1e-05
NEG = -1e30
BF = jnp.bfloat16
F32 = jnp.float32


def rope(vectors, positions):
    half = HEAD // 2
    powers = jnp.arange(half, dtype=F32) * (2.0 / HEAD)
    angles = positions.astype(F32)[..., None, None] * jnp.power(THETA, -powers)
    cos, sin = (jnp.cos(angles), jnp.sin(angles))
    lower, upper = (vectors[..., :half], vectors[..., half:])
    return jnp.concatenate([lower * cos - upper * sin, lower * sin + upper * cos], axis=-1)


def rms(rows, gain):
    return rows * lax.rsqrt(jnp.mean(rows * rows, axis=-1, keepdims=True) + EPS) * gain


def lineage_tables(parents):
    steps, groups, beams = parents.shape
    ident = jnp.broadcast_to(jnp.arange(beams, dtype=jnp.int32), (groups, beams))
    first = []
    tokens = [[None] * steps for _ in range(steps)]
    for t in range(steps):
        walker = ident
        for s in range(t, -1, -1):
            tokens[s][t] = walker
            hot = walker[..., None] == jnp.arange(beams, dtype=jnp.int32)
            walker = jnp.sum(jnp.where(hot, parents[s][:, None, :], 0), axis=-1)
        first.append(walker)
        for s in range(t + 1, steps):
            tokens[s][t] = jnp.full_like(ident, -1)
    return (jnp.stack(first), jnp.stack([jnp.stack(row) for row in tokens]))


def local(
    layer_in,
    query_in,
    key_in,
    value_in,
    prompt_keys,
    prompt_values,
    gen_keys,
    gen_values,
    lengths,
    parents,
    routes,
    sinks,
    out_weight,
    mlp_gain,
    router_weight,
    expert_gate,
    expert_up,
    expert_down,
    next_gain,
    next_q_weight,
    next_kv_weight,
):
    req_count = lax.axis_size("req")
    me = lax.axis_index("req")
    T, B, q_width = query_in.shape
    kv_width = key_in.shape[2]
    K = kv_width // HEAD
    R = q_width // kv_width
    J = parents.shape[2]
    span = req_count // J
    beam = me // span
    start = me % span * B
    groups = [[c + span * j for j in range(J)] for c in range(span)]
    if span == 1:
        groups = None
    lens = lax.dynamic_slice_in_dim(lengths, start, B)
    pars = lax.dynamic_slice_in_dim(parents, start, B, axis=1)
    S = prompt_keys.shape[1]
    G = gen_keys.shape[1]
    pos = lens[None, :] + G + jnp.arange(T, dtype=jnp.int32)[:, None]
    q = rope(query_in.astype(F32).reshape(T, B, K * R, HEAD), pos).astype(BF).reshape(T, B, q_width)
    k = rope(key_in.astype(F32).reshape(T, B, K, HEAD), pos).astype(BF).reshape(T, B, kv_width)
    q_all = lax.all_gather(q, "req", axis_index_groups=groups)
    first, tokens = lineage_tables(pars)
    prompt_ok = (beam * S + jnp.arange(S, dtype=jnp.int32))[None, :] < lens[:, None]
    mask = jnp.concatenate(
        [
            jnp.broadcast_to(prompt_ok[:, None, None, :], (B, J, T, S)),
            jnp.broadcast_to((first == beam).transpose(1, 2, 0)[..., None], (B, J, T, G)),
            (tokens == beam).transpose(2, 3, 1, 0),
        ],
        axis=-1,
    )
    keys = jnp.concatenate([prompt_keys, gen_keys, k.transpose(1, 0, 2)], axis=1)
    values = jnp.concatenate([prompt_values, gen_values, value_in.transpose(1, 0, 2)], axis=1)
    keys = keys.reshape(B, S + G + T, K, HEAD)
    values = values.reshape(B, S + G + T, K, HEAD)
    qs = q_all.reshape(J, T, B, K, R, HEAD)
    scores = jnp.einsum("jtbkrd,bskd->bkjtrs", qs, keys, preferred_element_type=F32) * 0.125
    usable = mask[:, None, :, :, None, :]
    scores = jnp.where(usable, scores, NEG)
    high = jnp.max(scores, axis=-1)
    weights = jnp.where(usable, jnp.exp(scores - high[..., None]), 0.0)
    total = jnp.sum(weights, axis=-1)
    part = jnp.einsum("bkjtrs,bskd->jtbkrd", weights.astype(BF), values, preferred_element_type=F32)
    high = high.transpose(2, 3, 0, 1, 4)
    total = total.transpose(2, 3, 0, 1, 4)
    part = (part / jnp.maximum(total, 1e-30)[..., None]).astype(BF)
    stats = jnp.stack([high, total], axis=1)
    part = lax.all_to_all(part, "req", 0, 0, axis_index_groups=groups)
    stats = lax.all_to_all(stats, "req", 0, 0, axis_index_groups=groups)
    high, total = (stats[:, 0], stats[:, 1])
    sink = sinks.reshape(K, R)
    peak = jnp.maximum(jnp.max(high, axis=0), sink)
    share = total * jnp.exp(high - peak)
    bottom = jnp.sum(share, axis=0) + jnp.exp(sink - peak)
    attended = jnp.sum(part.astype(F32) * (share / bottom)[..., None], axis=0)
    attended = attended.astype(BF).reshape(T * B, q_width)
    projected = jnp.dot(attended, out_weight, preferred_element_type=F32)
    x1 = layer_in.reshape(T * B, -1).astype(F32) + lax.psum(projected.astype(BF), "tp").astype(F32)
    h2 = rms(x1, mlp_gain).astype(BF)
    logits = jnp.dot(h2, router_weight, preferred_element_type=F32)
    hot = jnp.sum(
        (routes.reshape(T * B, -1, 1) == jnp.arange(EXPERTS, dtype=jnp.int32)).astype(F32), axis=1
    )
    masked = jnp.where(hot > 0, logits, NEG)
    raw = jnp.where(hot > 0, jnp.exp(masked - jnp.max(masked, axis=-1, keepdims=True)), 0.0)
    gates = raw / jnp.sum(raw, axis=-1, keepdims=True)
    h2_all = lax.all_gather(h2, "req", tiled=True)
    gates_all = lax.all_gather(gates, "req", tiled=True)
    slabs = expert_gate.shape[0]
    split = slabs * req_count // EXPERTS
    moe = 0.0
    for s in range(slabs):
        expert = (me * slabs + s) // split
        weight = lax.dynamic_slice_in_dim(gates_all, expert, 1, axis=1)
        gate = jnp.minimum(jnp.dot(h2_all, expert_gate[s], preferred_element_type=F32), 7.0)
        up = jnp.clip(jnp.dot(h2_all, expert_up[s], preferred_element_type=F32), -7.0, 7.0)
        hidden = ((up + 1.0) * gate * jax.nn.sigmoid(1.702 * gate) * weight).astype(BF)
        moe = moe + jnp.dot(hidden, expert_down[s], preferred_element_type=F32)
    moe = lax.psum_scatter(moe.astype(BF), "req", scatter_dimension=0, tiled=True)
    moe = lax.psum(moe, "tp").astype(F32)
    x2 = x1 + moe
    h3 = rms(x2, next_gain).astype(BF)
    next_query = jnp.dot(h3, next_q_weight, preferred_element_type=F32).astype(BF)
    next_kv = jnp.einsum("nd,dcf->ncf", h3, next_kv_weight, preferred_element_type=F32).astype(BF)
    return (
        x2.astype(BF).reshape(T, B, -1),
        next_query.reshape(T, B, q_width),
        next_kv.reshape(T, B, 2, kv_width),
    )


def solution(mesh):
    placed = (
        P(None, "req", None),
        P(None, "req", "tp"),
        P(None, "req", "tp"),
        P(None, "req", "tp"),
        P("req", None, "tp"),
        P("req", None, "tp"),
        P("req", None, "tp"),
        P("req", None, "tp"),
        P(),
        P(),
        P(None, "req", None),
        P("tp"),
        P("tp", None),
        P(),
        P(),
        P("req", None, "tp"),
        P("req", None, "tp"),
        P("req", "tp", None),
        P(),
        P(None, "tp"),
        P(None, None, "tp"),
    )
    return jax.shard_map(
        local,
        mesh=mesh,
        in_specs=placed,
        out_specs=(P(None, "req", None), P(None, "req", "tp"), P(None, "req", None, "tp")),
        check_vma=False,
    )
```

profile of v0, /device:TPU:0, one launch (start us, length us, event | category | flops | bytes accessed | tf_op | source)
XLA Modules:
  0.0 316.0 jit_solution(11140793845565401066)
XLA Ops:
  7.2 0.8 broadcast_add_fusion
  8.0 0.8 broadcast_compare_fusion.1
  8.8 0.7 slice_bitcast_fusion.4
  9.5 0.2 select_reduce_fusion.3
  9.8 0.4 select_reduce_fusion.6
  10.1 0.5 select_reduce_fusion.8
  10.7 0.7 select_reduce_fusion.9
  11.5 0.3 copy.117
  11.8 0.1 multiply_cosine_fusion
  12.0 0.8 reshape.192
  12.8 0.1 fusion.120
  12.9 0.1 pad_maximum_fusion.4
  13.0 0.1 convert_element_type.88
  13.1 0.9 reshape.190
  14.0 0.1 subtract_convert_fusion
  14.1 0.1 pad_maximum_fusion.3
  14.2 0.1 convert_element_type.87
  14.3 34.5 %all_gather.9 = bf16[8,4,8,512]{3,2,1,0:T(8,128)(2,1)} all-gather(bf16[1,4,8,512]{3,2,1,0:T(8,128)(2,1)S(1)} %convert_element_type.87), channel_id=1, replica_groups=mesh['req'=8,'tp'=4] {'req'}, dimensions={0}, use_global_device_ids=true | all-gather | bytes 294912 | tf_op jit(solution)/shard_map/all_gather | solution.py:88
  48.8 1.3 reshape.181
  50.1 2.0 pad_maximum_fusion.1
  52.1 2.2 copy.122
  54.4 0.1 broadcast_in_dim.144
  54.5 0.1 pad_add_fusion
  54.6 2.0 fusion.24
  56.7 1.6 copy-done.1
  58.3 1.3 fusion.25
  59.6 0.8 pad_maximum_fusion.2
  60.4 1.3 copy.125
  61.7 0.9 reshape.201
  62.6 5.5 %all-to-all-start.1 = ((f32[8,1,512]{2,1,0:T(1,128)}), f32[8,1,512]{2,1,0:T(1,128)S(1)}, u32[]{:S(2)}, u32[]{:S(2)}) async-start(f32[8,1,512]{2,1,0:T(1,128)} %reshape.201), calls=%async_computation.1 | async-start | bytes 32768 | tf_op jit(solution)/shard_map/all_to_all | solution.py:116
  68.1 2.0 pad_maximum_fusion
  70.1 2.2 copy.115
  72.4 3.9 %divide_convert_fusion = bf16[8,4,8,2,4,64]{5,0,4,1,3,2:T(8,128)(2,1)} fusion(bf16[8,324,2,64,1,1]{1,3,5,4,2,0:T(8,128)(2,1)} %bitcast.191, f32[8,2,8,4,4,324]{5,2,4,3,1,0:T(8,128)} %copy-done.1, f32[8,2,8,4,4]{2,4,3,1,0:T(4,128)S(1)} %copy-done.6, pred[8,8,4,324]{3,1,2,0:T(8,128)(4,1)} %copy-done.7, f32[8,4,8,2,4]{0,4,1,3,2:T(4,128)S(1)} %bitcast_maximum_fusion), kind=kOutput, calls=%fused_computation.55 | convolution fusion | flops 88514560 | bytes 3679232 | tf_op jit(solution)/shard_map/bkjtrs,bskd->jtbkrd/dot_general | solution.py:110
  76.3 1.2 copy.157
  77.6 1.1 reshape.199
  78.7 6.0 %all-to-all-start = ((bf16[8,2,8192]{2,1,0:T(2,128)(2,1)}), bf16[8,2,8192]{2,1,0:T(2,128)(2,1)}, u32[]{:S(2)}, u32[]{:S(2)}) async-start(bf16[8,2,8192]{2,1,0:T(2,128)(2,1)} %reshape.199), calls=%async_computation | async-start | bytes 524288 | tf_op jit(solution)/shard_map/all_to_all | solution.py:115
  84.7 0.5 broadcast.189
  85.2 0.7 reduce.1
  85.9 0.3 reshape.202
  86.4 0.1 fusion.119
  86.6 0.5 copy.127
  87.1 5.9 %all-to-all-done = bf16[8,2,8192]{2,1,0:T(2,128)(2,1)} async-done(((bf16[8,2,8192]{2,1,0:T(2,128)(2,1)}), bf16[8,2,8192]{2,1,0:T(2,128)(2,1)}, u32[]{:S(2)}, u32[]{:S(2)}) %all-to-all-start) | async-done | bytes 262176 | tf_op jit(solution)/shard_map/all_to_all | solution.py:115
  93.0 2.1 reshape.200
  95.1 1.7 multiply_reduce_fusion
  96.9 0.1 convert_element_type.93
  97.0 1.6 convolution_convert_fusion
  98.7 29.9 %all-reduce.3.cloned.1.call-done = bf16[32,2880]{1,0:T(8,128)(2,1)} async-done(((bf16[32,2880]{1,0:T(8,128)(2,1)}), bf16[32,2880]{1,0:T(8,128)(2,1)}) %all-reduce.3.cloned.1.call-update) | async-done | bytes 184336 | tf_op jit(solution)/shard_map/psum | solution.py:125
  128.6 1.1 multiply_reduce_fusion.2
  129.8 1.7 multiply_convert_fusion.1
  131.6 0.1 eq.163
  131.7 1.1 fusion.121
  132.8 30.8 %all-gather = f32[8,32,16]{1,2,0:T(8,128)S(1)} all-gather(f32[1,32,16]{1,2,0:T(8,128)S(1)} %divide_bitcast_fusion), channel_id=1, replica_groups=mesh['req'=8,'tp'=4] {'req'}, dimensions={0}, use_global_device_ids=true | all-gather | bytes 18432 | tf_op jit(solution)/shard_map/all_gather | solution.py:135
  163.8 11.5 %all-gather.3.cloned.1.call-done = bf16[256,2880]{1,0:T(8,128)(2,1)} async-done(((bf16[32,2880]{1,0:T(8,128)(2,1)}), bf16[256,2880]{1,0:T(8,128)(2,1)}) %all-gather.3.cloned.1.call-update) | async-done | bytes 1474576 | tf_op jit(solution)/shard_map/all_gather | solution.py:134
  175.3 5.0 %fusion.48 = f32[256,720]{0,1:T(8,128)} fusion(bf16[256,2880]{1,0:T(8,128)(2,1)} %all-gather.3.cloned.1.call-done, bf16[2,2880,720]{1,2,0:T(8,128)(2,1)} %param.36), kind=kOutput, calls=%fused_computation.38 | convolution fusion | flops 1061867520 | bytes 6483968 | tf_op jit(solution)/shard_map/dot_general | solution.py:142
  180.3 4.4 %fusion.42 = f32[256,720]{0,1:T(8,128)} fusion(bf16[256,2880]{1,0:T(8,128)(2,1)S(1)} %copy-done.13, bf16[2,2880,720]{1,2,0:T(8,128)(2,1)} %param.36), kind=kOutput, calls=%fused_computation.36 | convolution fusion | flops 1061867520 | bytes 6451200 | tf_op jit(solution)/shard_map/dot_general | solution.py:142
  184.7 10.7 %fusion = f32[256,2880]{1,0:T(8,128)} fusion(bf16[2,720,2880]{2,1,0:T(8,128)(2,1)} %param.38, f32[256,720]{0,1:T(8,128)} %fusion.48, bf16[256,2880]{1,0:T(8,128)(2,1)} %all-gather.3.cloned.1.call-done, bf16[2,2880,720]{1,2,0:T(8,128)(2,1)} %param.37, f32[256]{0:T(256)S(1)} %bitcast.205), kind=kOutput, calls=%fused_computation | convolution fusion | flops 2125209600 | bytes 13673472 | tf_op jit(solution)/shard_map/dot_general | solution.py:145
  195.3 11.1 %fusion.21 = bf16[256,2880]{1,0:T(8,128)(2,1)} fusion(f32[256,2880]{1,0:T(8,128)} %fusion, bf16[2,720,2880]{2,1,0:T(8,128)(2,1)} %param.38, f32[256,720]{0,1:T(8,128)} %fusion.42, bf16[256,2880]{1,0:T(8,128)(2,1)} %all-gather.3.cloned.1.call-done, bf16[2,2880,720]{1,2,0:T(8,128)(2,1)} %param.37, f32[256]{0:T(256)S(1)} %bitcast.204), kind=kOutput, calls=%fused_computation.19 | convolution fusion | flops 2126684160 | bytes 15213568 | tf_op jit(solution)/shard_map/dot_general | solution.py:145
  206.5 63.7 %reduce-scatter.2.cloned.1.call-done = bf16[32,2880]{1,0:T(8,128)(2,1)} async-done(((bf16[256,2880]{1,0:T(8,128)(2,1)}), bf16[32,2880]{1,0:T(8,128)(2,1)}) %reduce-scatter.2.cloned.1.call-update) | async-done | bytes 184336 | tf_op jit(solution)/shard_map/reduce_scatter | solution.py:146
  270.2 32.6 %all-reduce.5.cloned.1.call-done = bf16[32,2880]{1,0:T(8,128)(2,1)} async-done(((bf16[32,2880]{1,0:T(8,128)(2,1)}), bf16[32,2880]{1,0:T(8,128)(2,1)}) %all-reduce.5.cloned.1.call-update) | async-done | bytes 184336 | tf_op jit(solution)/shard_map/psum | solution.py:147
  302.9 1.3 multiply_reduce_fusion.1
  304.2 1.7 multiply_convert_fusion
  305.9 1.7 fusion.85
  307.6 1.2 fusion.81
  308.8 0.6 copy.133
  (72 shorter events, 1.1 us)
Async XLA Ops:
  7.2 89.8 %copy-start = (bf16[512,2880]{0,1:T(8,128)(2,1)S(1)}, bf16[512,2880]{0,1:T(8,128)(2,1)}, u32[]{:S(2)}) copy-start(bf16[512,2880]{0,1:T(8,128)(2,1)} %param.33) | copy-start | bytes 8847364
  54.6 5.0 %copy-start.7 = (pred[8,8,4,324]{3,1,2,0:T(8,128)(4,1)}, pred[8,8,4,324]{3,1,2,0:T(8,128)(4,1)S(1)}, u32[]{:S(2)}) copy-start(pred[8,8,4,324]{3,1,2,0:T(8,128)(4,1)S(1)} %pad_add_fusion) | copy-start | bytes 248836
  56.7 1.7 copy-start.1
  56.7 2.9 copy-start.5
  56.7 11.4 %copy-start.11 = (bf16[4,8,128]{2,1,0:T(8,128)(2,1)S(1)}, bf16[4,8,128]{2,1,0:T(8,128)(2,1)}, u32[]{:S(2)}) copy-start(bf16[4,8,128]{2,1,0:T(8,128)(2,1)} %param.24) | copy-start | bytes 24580
  60.4 12.0 %copy-start.6 = (f32[8,2,8,4,4]{2,4,3,1,0:T(4,128)S(1)}, f32[8,2,8,4,4]{2,4,3,1,0:T(4,128)}, u32[]{:S(2)}) copy-start(f32[8,2,8,4,4]{2,4,3,1,0:T(4,128)} %copy-done.5) | copy-start | bytes 24580
  62.6 16.1 %all-to-all-start.1 = ((f32[8,1,512]{2,1,0:T(1,128)}), f32[8,1,512]{2,1,0:T(1,128)S(1)}, u32[]{:S(2)}, u32[]{:S(2)}) async-start(f32[8,1,512]{2,1,0:T(1,128)} %reshape.201), calls=%async_computation.1 | async-start | bytes 32768 | tf_op jit(solution)/shard_map/all_to_all | solution.py:116
  72.4 3.9 %copy-start.14 = (f32[8]{0:T(128)S(1)}, f32[8]{0:T(128)}, u32[]{:S(2)}) copy-start(f32[8]{0:T(128)} %param.32) | copy-start | bytes 100
  78.7 14.3 %all-to-all-start = ((bf16[8,2,8192]{2,1,0:T(2,128)(2,1)}), bf16[8,2,8192]{2,1,0:T(2,128)(2,1)}, u32[]{:S(2)}, u32[]{:S(2)}) async-start(bf16[8,2,8192]{2,1,0:T(2,128)(2,1)} %reshape.199), calls=%async_computation | async-start | bytes 524288 | tf_op jit(solution)/shard_map/all_to_all | solution.py:115
  84.7 44.0 %all-reduce.3.cloned.1.call-start = ((), (), s32[]{:S(2)}) async-start(), calls=%async_computation.3 | async-start | bytes 376832 | tf_op jit(solution)/shard_map/psum | solution.py:125
  86.4 42.3 %copy-start.2 = (bf16[4,8,2880]{2,1,0:T(8,128)(2,1)S(1)}, bf16[4,8,2880]{2,1,0:T(8,128)(2,1)}, u32[]{:S(2)}) copy-start(bf16[4,8,2880]{2,1,0:T(8,128)(2,1)} %param.21) | copy-start | bytes 552964
  86.6 43.2 %copy-start.10 = (f32[2880]{0:T(1024)S(1)}, f32[2880]{0:T(1024)}, u32[]{:S(2)}) copy-start(f32[2880]{0:T(1024)} %param.34) | copy-start | bytes 34564
  87.1 44.5 %copy-start.12 = (s32[4,8,4]{1,2,0:T(4,128)S(1)}, s32[4,8,4]{1,2,0:T(4,128)}, u32[]{:S(2)}) copy-start(s32[4,8,4]{1,2,0:T(4,128)} %param.31) | copy-start | bytes 1540
  87.1 44.6 %copy-start.8 = (bf16[2880,16]{0,1:T(8,128)(2,1)S(1)}, bf16[2880,16]{0,1:T(8,128)(2,1)}, u32[]{:S(2)}) copy-start(bf16[2880,16]{0,1:T(8,128)(2,1)} %param.35) | copy-start | bytes 276484
  98.6 76.6 %all-gather.3.cloned.1.call-start = ((), (), s32[]{:S(2)}) async-start(), calls=%async_computation.4 | async-start | bytes 1695744 | tf_op jit(solution)/shard_map/all_gather | solution.py:134
  131.5 138.7 %reduce-scatter.2.cloned.1.call-start = ((), (), s32[]{:S(2)}) async-start(), calls=%async_computation.5 | async-start | bytes 1695744 | tf_op jit(solution)/shard_map/reduce_scatter | solution.py:146
  175.3 5.0 %copy-start.13 = (bf16[256,2880]{1,0:T(8,128)(2,1)S(1)}, bf16[256,2880]{1,0:T(8,128)(2,1)}, u32[]{:S(2)}) copy-start(bf16[256,2880]{1,0:T(8,128)(2,1)} %all-gather.3.cloned.1.call-done) | copy-start | bytes 4423684
  195.3 107.5 %copy-start.3 = (bf16[32,2880]{1,0:T(8,128)(2,1)S(1)}, bf16[32,2880]{1,0:T(8,128)(2,1)}, u32[]{:S(2)}) copy-start(bf16[32,2880]{1,0:T(8,128)(2,1)} %all-reduce.3.cloned.1.call-done) | copy-start | bytes 552964
  195.3 108.8 %copy-start.9 = (f32[2880]{0:T(1024)S(1)}, f32[2880]{0:T(1024)}, u32[]{:S(2)}) copy-start(f32[2880]{0:T(1024)} %param.39) | copy-start | bytes 34564
  206.4 96.4 %all-reduce.5.cloned.1.call-start = ((), (), s32[]{:S(2)}) async-start(), calls=%async_computation.6 | async-start | bytes 376832 | tf_op jit(solution)/shard_map/psum | solution.py:147
  302.9 4.8 %copy-start.4 = (bf16[2880,512]{1,0:T(8,128)(2,1)S(1)}, bf16[2880,512]{1,0:T(8,128)(2,1)}, u32[]{:S(2)}) copy-start(bf16[2880,512]{1,0:T(8,128)(2,1)} %param.40) | copy-start | bytes 8847364
Sparse Core Ops, SparseCore 0:
  98.8 29.8 all-reduce.2
  131.6 43.5 all-gather.2
  206.6 63.5 reduce-scatter.1
  272.4 30.4 all-reduce.4
where the time goes:
time: 317 us; the launch traced here: 316 us
  waiting for transfers between devices  144 us (45%)
  blocking collectives  65.4 us (21%)
  matrix products  42.8 us (14%)
  local copies, waits for them, and re-layouts  19.6 us (6%)
  other arithmetic  18.8 us (6%)
  between operations  14.2 us (4%)
  starting transfers between devices  11.6 us (4%)
    reduce_scatter x1, waiting for transfers between devices, local(): lax.psum_scatter(moe.astype(BF), 'req', scatter_dimension=0, tiled=True)  63.7 us
    all_gather x1, blocking collectives, local(): q_all = lax.all_gather(q, 'req', axis_index_groups=groups)  34.5 us
    psum x1, waiting for transfers between devices, local(): moe = lax.psum(moe, 'tp').astype(F32)  32.6 us
    all_gather x1, blocking collectives, local(): gates_all = lax.all_gather(gates, 'req', tiled=True)  30.8 us
    psum x1, waiting for transfers between devices, local(): lax.psum(projected.astype(BF), 'tp').astype(F32)  29.9 us
    dot_general x2, matrix products, local(): moe = moe + jnp.dot(hidden, expert_down[s], preferred_element_type=F32)  21.7 us
    all_gather x1, waiting for transfers between devices, local(): h2_all = lax.all_gather(h2, 'req', tiled=True)  11.5 us
    dot_general x2, matrix products, local(): jnp.dot(h2_all, expert_gate[s], preferred_element_type=F32)  9.4 us
  transfers between devices with their start and end apart: 6, of which 5 were waited for; matrix products, arithmetic and copies ran while one was open for 5% of the time, Pallas kernels for 0%

commit v1 on v0

--- a/solution.py
+++ b/solution.py
@@ -131,8 +131,11 @@
     masked = jnp.where(hot > 0, logits, NEG)
     raw = jnp.where(hot > 0, jnp.exp(masked - jnp.max(masked, axis=-1, keepdims=True)), 0.0)
     gates = raw / jnp.sum(raw, axis=-1, keepdims=True)
-    h2_all = lax.all_gather(h2, "req", tiled=True)
-    gates_all = lax.all_gather(gates, "req", tiled=True)
+    h2_all, gates_all = jnp.split(
+        lax.all_gather(jnp.concatenate([h2, gates], axis=1), "req", tiled=True),
+        [h2.shape[1]],
+        axis=1,
+    )
     slabs = expert_gate.shape[0]
     split = slabs * req_count // EXPERTS
     moe = 0.0

time: 317 us -> 337 us (1.063)
  waiting for transfers between devices: 144 us -> 191 us
  blocking collectives: 65.4 us -> 34.5 us
    all_gather x1, waiting for transfers between devices: 11.5 us -> 59.1 us  [local(): lax.all_gather(jnp.concatenate([h2, gates], axis=1), 'req', tiled=True)]
    all_gather x1 -> x0, blocking collectives: 30.8 us -> none  [local(): gates_all = lax.all_gather(gates, 'req', tiled=True)]
    unnamed x38 -> x37, local copies, waits for them, and re-layouts: 6.82 us -> 6.74 us
  transfers between devices with their start and end apart: 6 -> 6, of which waited for: 5 -> 5; matrix products, arithmetic and copies ran while one was open for 5% -> 4% of each run, Pallas kernels for 0% -> 0%
where the time goes in v1:
time: 337 us; the launch traced here: 336 us
  waiting for transfers between devices  191 us (57%)
  matrix products  44.3 us (13%)
  blocking collectives  34.5 us (10%)
  local copies, waits for them, and re-layouts  20.8 us (6%)
  other arithmetic  19.2 us (6%)
  between operations  14.2 us (4%)
  starting transfers between devices  11.8 us (4%)
    reduce_scatter x1, waiting for transfers between devices, local(): lax.psum_scatter(moe.astype(BF), 'req', scatter_dimension=0, tiled=True)  63.6 us
    all_gather x1, waiting for transfers between devices, local(): lax.all_gather(jnp.concatenate([h2, gates], axis=1), 'req', tiled=True)  59.1 us
    all_gather x1, blocking collectives, local(): q_all = lax.all_gather(q, 'req', axis_index_groups=groups)  34.5 us
    psum x1, waiting for transfers between devices, local(): moe = lax.psum(moe, 'tp').astype(F32)  32.7 us
    psum x1, waiting for transfers between devices, local(): lax.psum(projected.astype(BF), 'tp').astype(F32)  29.9 us
    dot_general x2, matrix products, local(): moe = moe + jnp.dot(hidden, expert_down[s], preferred_element_type=F32)  22.6 us
    dot_general x2, matrix products, local(): jnp.dot(h2_all, expert_gate[s], preferred_element_type=F32)  9.88 us
  transfers between devices with their start and end apart: 6, of which 5 were waited for; matrix products, arithmetic and copies ran while one was open for 4% of the time, Pallas kernels for 0%

profile of v1, /device:TPU:0, one launch (start us, length us, event | category | flops | bytes accessed | tf_op | source)
XLA Modules:
  0.0 335.9 jit_solution(14099005123915770695)
XLA Ops:
  7.2 0.8 broadcast_add_fusion
  8.0 0.8 broadcast_compare_fusion.1
  8.8 0.7 slice_bitcast_fusion.4
  9.5 0.2 select_reduce_fusion.3
  9.8 0.4 select_reduce_fusion.6
  10.1 0.5 select_reduce_fusion.8
  10.7 0.7 select_reduce_fusion.9
  11.5 0.3 copy.118
  11.8 0.1 multiply_cosine_fusion
  12.0 0.8 reshape.192
  12.9 0.1 pad_maximum_fusion.5
  13.1 0.9 reshape.190
  14.0 0.1 subtract_convert_fusion
  14.1 0.1 pad_maximum_fusion.4
  14.2 0.1 convert_element_type.90
  14.3 34.5 %all_gather.6 = bf16[8,4,8,512]{3,2,1,0:T(8,128)(2,1)} all-gather(bf16[1,4,8,512]{3,2,1,0:T(8,128)(2,1)S(1)} %convert_element_type.90), channel_id=1, replica_groups=mesh['req'=8,'tp'=4] {'req'}, dimensions={0}, use_global_device_ids=true | all-gather | bytes 294912 | tf_op jit(solution)/shard_map/all_gather | solution.py:88
  48.8 1.3 reshape.181
  50.1 2.0 pad_maximum_fusion.1
  52.1 2.2 copy.123
  54.4 0.1 broadcast_in_dim.144
  54.5 0.1 pad_add_fusion
  54.6 2.0 fusion.24
  56.7 1.6 copy-done.1
  58.3 1.3 fusion.29
  59.6 0.8 pad_maximum_fusion.3
  60.4 1.3 copy.126
  61.7 0.9 reshape.201
  62.6 5.5 %all-to-all-start.1 = ((f32[8,1,512]{2,1,0:T(1,128)}), f32[8,1,512]{2,1,0:T(1,128)S(1)}, u32[]{:S(2)}, u32[]{:S(2)}) async-start(f32[8,1,512]{2,1,0:T(1,128)} %reshape.201), calls=%async_computation.1 | async-start | bytes 32768 | tf_op jit(solution)/shard_map/all_to_all | solution.py:116
  68.1 2.0 pad_maximum_fusion
  70.1 2.2 copy.116
  72.4 3.9 %divide_convert_fusion = bf16[8,4,8,2,4,64]{5,0,4,1,3,2:T(8,128)(2,1)} fusion(bf16[8,324,2,64,1,1]{1,3,5,4,2,0:T(8,128)(2,1)} %bitcast.185, f32[8,2,8,4,4,324]{5,2,4,3,1,0:T(8,128)} %copy-done.1, f32[8,2,8,4,4]{2,4,3,1,0:T(4,128)S(1)} %copy-done.6, pred[8,8,4,324]{3,1,2,0:T(8,128)(4,1)} %copy-done.7, f32[8,4,8,2,4]{0,4,1,3,2:T(4,128)S(1)} %bitcast_maximum_fusion), kind=kOutput, calls=%fused_computation.59 | convolution fusion | flops 88514560 | bytes 3679232 | tf_op jit(solution)/shard_map/bkjtrs,bskd->jtbkrd/dot_general | solution.py:110
  76.4 1.2 copy.160
  77.7 1.1 reshape.199
  78.8 6.0 %all-to-all-start = ((bf16[8,2,8192]{2,1,0:T(2,128)(2,1)}), bf16[8,2,8192]{2,1,0:T(2,128)(2,1)}, u32[]{:S(2)}, u32[]{:S(2)}) async-start(bf16[8,2,8192]{2,1,0:T(2,128)(2,1)} %reshape.199), calls=%async_computation | async-start | bytes 524288 | tf_op jit(solution)/shard_map/all_to_all | solution.py:115
  84.8 0.5 broadcast.193
  85.3 0.7 reduce.5
  86.0 0.3 reshape.202
  86.7 0.5 copy.128
  87.2 5.9 %all-to-all-done = bf16[8,2,8192]{2,1,0:T(2,128)(2,1)} async-done(((bf16[8,2,8192]{2,1,0:T(2,128)(2,1)}), bf16[8,2,8192]{2,1,0:T(2,128)(2,1)}, u32[]{:S(2)}, u32[]{:S(2)}) %all-to-all-start) | async-done | bytes 262176 | tf_op jit(solution)/shard_map/all_to_all | solution.py:115
  93.1 2.1 reshape.200
  95.2 1.7 multiply_reduce_fusion
  97.0 0.1 convert_element_type.96
  97.1 1.6 convolution_convert_fusion
  98.9 29.9 %all-reduce.3.cloned.1.call-done = bf16[32,2880]{1,0:T(8,128)(2,1)} async-done(((bf16[32,2880]{1,0:T(8,128)(2,1)}), bf16[32,2880]{1,0:T(8,128)(2,1)}) %all-reduce.3.cloned.1.call-update) | async-done | bytes 184336 | tf_op jit(solution)/shard_map/psum | solution.py:125
  128.8 1.1 multiply_reduce_fusion.2
  129.9 1.3 fusion.163
  131.2 0.2 fusion.148
  131.5 1.0 fusion.161
  132.5 0.8 pad_maximum_fusion.2
  133.4 0.2 reduce-scatter.2.cloned.1.call-start
  133.6 59.1 %all-gather.2.cloned.1.call-done = f32[256,2896]{1,0:T(8,128)} async-done(((f32[32,2896]{1,0:T(8,128)}), f32[256,2896]{1,0:T(8,128)}) %all-gather.2.cloned.1.call-update) | async-done | bytes 2965520 | tf_op jit(solution)/shard_map/all_gather | solution.py:135
  192.7 1.0 split.9
  193.7 0.3 dynamic-slice_reduce_fusion.1
  193.9 5.5 %fusion.48 = f32[256,720]{0,1:T(8,128)} fusion(bf16[2,2880,720]{1,2,0:T(8,128)(2,1)} %param.36, f32[256,2896]{1,0:T(8,128)} %all-gather.2.cloned.1.call-done), kind=kOutput, calls=%fused_computation.40 | convolution fusion | flops 1061867520 | bytes 6483968 | tf_op jit(solution)/shard_map/dot_general | solution.py:145
  199.4 4.4 %fusion.58 = f32[256,720]{0,1:T(8,128)} fusion(bf16[2,2880,720]{1,2,0:T(8,128)(2,1)} %param.36, f32[256,2896]{1,0:T(8,128)S(1)} %copy-done.12), kind=kOutput, calls=%fused_computation.42 | convolution fusion | flops 1061867520 | bytes 6483968 | tf_op jit(solution)/shard_map/dot_general | solution.py:145
  203.8 11.1 %fusion = f32[256,2880]{1,0:T(8,128)} fusion(bf16[2,720,2880]{2,1,0:T(8,128)(2,1)} %param.38, f32[256,720]{0,1:T(8,128)} %fusion.58, bf16[2,2880,720]{1,2,0:T(8,128)(2,1)} %param.37, f32[256,2896]{1,0:T(8,128)} %all-gather.2.cloned.1.call-done, f32[256]{0:T(256)S(1)} %get-tuple-element.22), kind=kOutput, calls=%fused_computation | convolution fusion | flops 2125209600 | bytes 13673472 | tf_op jit(solution)/shard_map/dot_general | solution.py:148
  214.9 11.5 %fusion.21 = bf16[256,2880]{1,0:T(8,128)(2,1)} fusion(f32[256,2880]{1,0:T(8,128)} %fusion, bf16[2,720,2880]{2,1,0:T(8,128)(2,1)} %param.38, f32[256,720]{0,1:T(8,128)} %fusion.48, bf16[2,2880,720]{1,2,0:T(8,128)(2,1)} %param.37, f32[256,2896]{1,0:T(8,128)} %all-gather.2.cloned.1.call-done, f32[256]{0:T(256)S(1)} %get-tuple-element.21), kind=kOutput, calls=%fused_computation.19 | convolution fusion | flops 2126684160 | bytes 15213568 | tf_op jit(solution)/shard_map/dot_general | solution.py:148
  226.5 63.6 %reduce-scatter.2.cloned.1.call-done = bf16[32,2880]{1,0:T(8,128)(2,1)} async-done(((bf16[256,2880]{1,0:T(8,128)(2,1)}), bf16[32,2880]{1,0:T(8,128)(2,1)}) %reduce-scatter.2.cloned.1.call-update) | async-done | bytes 184336 | tf_op jit(solution)/shard_map/reduce_scatter | solution.py:149
  290.1 32.7 %all-reduce.5.cloned.1.call-done = bf16[32,2880]{1,0:T(8,128)(2,1)} async-done(((bf16[32,2880]{1,0:T(8,128)(2,1)}), bf16[32,2880]{1,0:T(8,128)(2,1)}) %all-reduce.5.cloned.1.call-update) | async-done | bytes 184336 | tf_op jit(solution)/shard_map/psum | solution.py:150
  322.8 1.3 multiply_reduce_fusion.1
  324.1 1.7 multiply_convert_fusion
  325.8 1.7 fusion.117
  327.5 1.2 fusion.113
  328.7 0.6 copy.135
  (72 shorter events, 1.4 us)
Async XLA Ops:
  7.2 89.9 %copy-start = (bf16[512,2880]{0,1:T(8,128)(2,1)S(1)}, bf16[512,2880]{0,1:T(8,128)(2,1)}, u32[]{:S(2)}) copy-start(bf16[512,2880]{0,1:T(8,128)(2,1)} %param.33) | copy-start | bytes 8847364
  54.6 5.0 %copy-start.7 = (pred[8,8,4,324]{3,1,2,0:T(8,128)(4,1)}, pred[8,8,4,324]{3,1,2,0:T(8,128)(4,1)S(1)}, u32[]{:S(2)}) copy-start(pred[8,8,4,324]{3,1,2,0:T(8,128)(4,1)S(1)} %pad_add_fusion) | copy-start | bytes 248836
  56.7 1.7 copy-start.1
  56.7 2.9 copy-start.5
  56.7 11.4 %copy-start.10 = (bf16[4,8,128]{2,1,0:T(8,128)(2,1)S(1)}, bf16[4,8,128]{2,1,0:T(8,128)(2,1)}, u32[]{:S(2)}) copy-start(bf16[4,8,128]{2,1,0:T(8,128)(2,1)} %param.24) | copy-start | bytes 24580
  60.4 12.0 %copy-start.6 = (f32[8,2,8,4,4]{2,4,3,1,0:T(4,128)S(1)}, f32[8,2,8,4,4]{2,4,3,1,0:T(4,128)}, u32[]{:S(2)}) copy-start(f32[8,2,8,4,4]{2,4,3,1,0:T(4,128)} %copy-done.5) | copy-start | bytes 24580
  62.6 16.2 %all-to-all-start.1 = ((f32[8,1,512]{2,1,0:T(1,128)}), f32[8,1,512]{2,1,0:T(1,128)S(1)}, u32[]{:S(2)}, u32[]{:S(2)}) async-start(f32[8,1,512]{2,1,0:T(1,128)} %reshape.201), calls=%async_computation.1 | async-start | bytes 32768 | tf_op jit(solution)/shard_map/all_to_all | solution.py:116
  72.4 3.9 %copy-start.14 = (f32[8]{0:T(128)S(1)}, f32[8]{0:T(128)}, u32[]{:S(2)}) copy-start(f32[8]{0:T(128)} %param.32) | copy-start | bytes 100
  72.4 4.0 %copy-start.11 = (s32[4,8,4]{1,2,0:T(4,128)S(1)}, s32[4,8,4]{1,2,0:T(4,128)}, u32[]{:S(2)}) copy-start(s32[4,8,4]{1,2,0:T(4,128)} %param.31) | copy-start | bytes 1540
  78.8 14.3 %all-to-all-start = ((bf16[8,2,8192]{2,1,0:T(2,128)(2,1)}), bf16[8,2,8192]{2,1,0:T(2,128)(2,1)}, u32[]{:S(2)}, u32[]{:S(2)}) async-start(bf16[8,2,8192]{2,1,0:T(2,128)(2,1)} %reshape.199), calls=%async_computation | async-start | bytes 524288 | tf_op jit(solution)/shard_map/all_to_all | solution.py:115
  84.8 44.0 %all-reduce.3.cloned.1.call-start = ((), (), s32[]{:S(2)}) async-start(), calls=%async_computation.3 | async-start | bytes 376832 | tf_op jit(solution)/shard_map/psum | solution.py:125
  86.5 42.3 %copy-start.2 = (bf16[4,8,2880]{2,1,0:T(8,128)(2,1)S(1)}, bf16[4,8,2880]{2,1,0:T(8,128)(2,1)}, u32[]{:S(2)}) copy-start(bf16[4,8,2880]{2,1,0:T(8,128)(2,1)} %param.21) | copy-start | bytes 552964
  86.7 43.2 %copy-start.9 = (f32[2880]{0:T(1024)S(1)}, f32[2880]{0:T(1024)}, u32[]{:S(2)}) copy-start(f32[2880]{0:T(1024)} %param.34) | copy-start | bytes 34564
  87.2 42.7 %copy-start.13 = (bf16[2880,16]{0,1:T(8,128)(2,1)S(1)}, bf16[2880,16]{0,1:T(8,128)(2,1)}, u32[]{:S(2)}) copy-start(bf16[2880,16]{0,1:T(8,128)(2,1)} %param.35) | copy-start | bytes 276484
  98.8 93.9 %all-gather.2.cloned.1.call-start = ((), (), s32[]{:S(2)}) async-start(), calls=%async_computation.4 | async-start | bytes 3391488 | tf_op jit(solution)/shard_map/all_gather | solution.py:135
  133.4 156.7 %reduce-scatter.2.cloned.1.call-start = ((), (), s32[]{:S(2)}) async-start(), calls=%async_computation.5 | async-start | bytes 1695744 | tf_op jit(solution)/shard_map/reduce_scatter | solution.py:149
  193.9 5.5 %copy-start.12 = (f32[256,2896]{1,0:T(8,128)S(1)}, f32[256,2896]{1,0:T(8,128)}, u32[]{:S(2)}) copy-start(f32[256,2896]{1,0:T(8,128)} %all-gather.2.cloned.1.call-done) | copy-start | bytes 8896516
  214.9 107.8 %copy-start.3 = (bf16[32,2880]{1,0:T(8,128)(2,1)S(1)}, bf16[32,2880]{1,0:T(8,128)(2,1)}, u32[]{:S(2)}) copy-start(bf16[32,2880]{1,0:T(8,128)(2,1)} %all-reduce.3.cloned.1.call-done) | copy-start | bytes 552964
  214.9 109.1 %copy-start.8 = (f32[2880]{0:T(1024)S(1)}, f32[2880]{0:T(1024)}, u32[]{:S(2)}) copy-start(f32[2880]{0:T(1024)} %param.39) | copy-start | bytes 34564
  226.4 96.3 %all-reduce.5.cloned.1.call-start = ((), (), s32[]{:S(2)}) async-start(), calls=%async_computation.6 | async-start | bytes 376832 | tf_op jit(solution)/shard_map/psum | solution.py:150
  322.8 4.8 %copy-start.4 = (bf16[2880,512]{1,0:T(8,128)(2,1)S(1)}, bf16[2880,512]{1,0:T(8,128)(2,1)}, u32[]{:S(2)}) copy-start(bf16[2880,512]{1,0:T(8,128)(2,1)} %param.40) | copy-start | bytes 8847364
Sparse Core Ops, SparseCore 0:
  98.9 29.8 all-reduce.2
  133.5 59.1 all-gather.1
  226.6 63.4 reduce-scatter.1
  292.2 30.4 all-reduce.4
